TPU v7x, 256 devices: a whole 4x4x8 slice. The times are simulated.
256 devices in a mesh: tm: 32 (over z_hi, y, core), seq: 8 (over x, z_lo).
Axes of the slice: x: 4, y: 4, z: 8 (z_hi: 4, z_lo: 2; z = z_hi * 2 + z_lo), core: 2. Of those that a mesh axis runs over, the one named last changes fastest.
Arguments:
- projected: bfloat16 [32, 1024, 3, 3072], P('tm', 'seq'), may hold values from -32 to 32
- residual: bfloat16 [32, 1024, 3072], P('tm', 'seq'), may hold values from -3 to 3
- timesteps: int32 [32], P('tm'), may hold values from 0 to 49
- gate_table: float32 [50, 3072], replicated, may hold values from 0.2 to 2
- out_weight: bfloat16 [3072, 3072], P(('tm', 'seq')), may hold values from -0.4375 to 0.4375
Outputs:
- block_out: bfloat16 [32, 1024, 3072], P('tm', 'seq')
All inputs are finite; a program needn't handle non-finite values.
Results may differ from a plain program's by a relative error of at most 0.0052.
Values may be sent and summed in bfloat16 or wider, within the bound.
A program may use at most 128 MiB of HBM per device.

v0:
```python
import math

import jax
import jax.numpy as jnp
from jax import lax
from jax.sharding import PartitionSpec as P

HEAD_DIM = 128


def attend(local):
    seq_len = local.shape[0]
    width = local.shape[2]
    nheads = width // HEAD_DIM
    split_heads = local.reshape(seq_len, 3, nheads, HEAD_DIM)
    queries = split_heads[:, 0]
    keys = split_heads[:, 1]
    values = split_heads[:, 2]
    block_rows = min(512, seq_len)
    scale = 1.0 / math.sqrt(HEAD_DIM)
    query_blocks = queries.reshape(seq_len // block_rows, block_rows, nheads, HEAD_DIM)

    def one_block(query_block):
        scores = (
            jnp.einsum("qhd,khd->hqk", query_block, keys, preferred_element_type=jnp.float32)
            * scale
        )
        top = jnp.max(scores, axis=-1, keepdims=True)
        weights = jnp.exp(scores - top)
        totals = jnp.sum(weights, axis=-1, keepdims=True)
        probs = weights.astype(jnp.bfloat16)
        summed = jnp.einsum("hqk,khd->qhd", probs, values, preferred_element_type=jnp.float32)
        normed = summed / totals.transpose(1, 0, 2)
        return normed.astype(jnp.bfloat16).reshape(block_rows, width)

    return lax.map(one_block, query_blocks).reshape(seq_len, width)


def shards(projected, residual, timesteps, gate_table, out_weight):
    local = lax.all_to_all(projected, "seq", split_axis=3, concat_axis=1, tiled=True)
    attended = attend(local[0])
    seq_len = attended.shape[0]
    step_count = gate_table.shape[0]
    selector = (jnp.arange(step_count) == timesteps[0]).astype(jnp.float32)
    gate = jnp.dot(selector, gate_table, precision=lax.Precision.HIGHEST)
    back = lax.all_to_all(
        attended.reshape(1, seq_len, attended.shape[1]),
        "seq",
        split_axis=1,
        concat_axis=2,
        tiled=True,
    )[0]
    product = jnp.dot(
        back,
        lax.all_gather(out_weight, ("tm", "seq"), axis=0, tiled=True),
        preferred_element_type=jnp.float32,
    )
    result = residual[0].astype(jnp.float32) + gate[None, :] * product
    return result.astype(jnp.bfloat16)[None]


def solution(mesh):
    placed = (
        P("tm", "seq", None, None),
        P("tm", "seq", None),
        P("tm"),
        P(),
        P(("tm", "seq"), None),
    )
    return jax.shard_map(
        shards, mesh=mesh, in_specs=placed, out_specs=P("tm", "seq", None), check_vma=False
    )
```

profile of v0, /device:TPU:33, one launch (start us, length us, event | category | flops | bytes accessed | tf_op | source)
XLA Modules:
  0.0 812.0 jit_solution(6877053336732147704)
XLA Ops:
  6.5 0.7 all-gather.3.cloned.1.call-update
  7.3 5.7 copy.24
  12.9 5.2 all-to-all-start
  18.1 38.1 %all-to-all-done = bf16[1,128,3,3072]{1,2,0,3:T(4,128)(2,1)} async-done(((bf16[1,128,3,3072]{1,2,0,3:T(4,128)(2,1)}), bf16[1,128,3,3072]{1,2,0,3:T(4,128)(2,1)}, u32[]{:S(2)}, u32[]{:S(2)}) %all-to-all-start) | async-done | bytes 2359328 | tf_op jit(solution)/shard_map/all_to_all | solution.py:40
  56.2 5.3 copy.38
  61.5 3.6 reshape_squeeze.6
  65.2 1.5 slice_bitcast_fusion
  66.7 1.5 copy.27
  68.2 1.5 copy.26
  69.7 9.8 %while.10 = (s32[]{:T(128)}, bf16[2,512,384]{2,1,0:T(8,128)(2,1)}, bf16[2,512,3,128]{3,1,0,2:T(8,128)(2,1)S(1)}, bf16[1024,3,128]{2,0,1:T(8,128)(2,1)S(1)}, bf16[1024,3,128]{0,2,1:T(8,128)(2,1)}, /*index=5*/s32[]{:T(128)}) while((s32[]{:T(128)}, bf16[2,512,384]{2,1,0:T(8,128)(2,1)}, bf16[2,512,3,128]{3,1,0,2:T(8,128)(2,1)S(1)}, ...), condition=%wide.region_3.4_spmd, body=%wide.region_0.3_spmd.sunk | while | flops 818279424 | bytes 25983088 | solution.py:36
  69.8 1.1 multiply_reduce_fusion.2
  70.8 1.3 fusion.41
  72.2 1.5 fusion.42
  73.7 0.2 copy.41
  73.9 0.8 constant_dynamic-update-slice_fusion.2
  74.7 1.1 multiply_reduce_fusion.2
  75.7 1.3 fusion.41
  77.1 1.5 fusion.42
  78.6 0.2 copy.41
  78.8 0.8 constant_dynamic-update-slice_fusion.2
  79.6 2.4 copy.39
  81.9 0.5 broadcast.17
  82.4 5.4 reduce
  87.9 1.1 reshape.13
  89.0 5.3 all-to-all-start.1
  94.9 0.3 fusion.23
  95.3 11.5 %all-to-all-done.1 = bf16[8,2,24576]{2,1,0:T(2,128)(2,1)S(1)} async-done(((bf16[8,2,24576]{2,1,0:T(2,128)(2,1)}), bf16[8,2,24576]{2,1,0:T(2,128)(2,1)S(1)}, u32[]{:S(2)}, u32[]{:S(2)}) %all-to-all-start.1) | async-done | bytes 786464 | tf_op jit(solution)/shard_map/all_to_all | solution.py:46
  106.8 0.8 reshape.14
  107.7 0.4 copy.31
  108.1 661.1 %all-gather.3.cloned.1.call-done = bf16[256,12,3072]{2,1,0:T(8,128)(2,1)} async-done(((bf16[1,12,3072]{2,1,0:T(8,128)(2,1)}), bf16[256,12,3072]{2,1,0:T(8,128)(2,1)}) %all-gather.3.cloned.1.call-update) | async-done | bytes 18874384 | tf_op jit(solution)/shard_map/all_gather | solution.py:55
  769.2 26.0 %reshape.10 = bf16[3072,3072]{1,0:T(8,128)(2,1)} reshape(bf16[256,12,3072]{2,1,0:T(8,128)(2,1)} %all-gather.3.cloned.1.call-done) | data formatting | bytes 37748736
  795.3 9.9 %fusion.22 = bf16[1,128,3072]{2,1,0:T(8,128)(2,1)} fusion(bf16[128,3072]{0,1:T(8,128)(2,1)S(1)} %bitcast.75, bf16[3072,3072]{1,0:T(8,128)(2,1)} %reshape.10, bf16[1,128,3072]{2,1,0:T(8,128)(2,1)S(1)} %copy-done.1, f32[3072]{0:T(1024)S(1)} %bitcast.80), kind=kOutput, calls=%fused_computation.19 | convolution fusion | flops 2417491968 | bytes 21245952 | tf_op jit(solution)/shard_map/dot_general | solution.py:53
  (11 shorter events, 0.1 us)
Async XLA Ops:
  6.5 88.4 %copy-start = (f32[50,3072]{1,0:T(8,128)S(1)}, f32[50,3072]{1,0:T(8,128)}, u32[]{:S(2)}) copy-start(f32[50,3072]{1,0:T(8,128)} %param.10) | copy-start | bytes 1843204
  6.5 762.7 %all-gather.3.cloned.1.call-start = ((), (), s32[]{:S(2)}) async-start(), calls=%async_computation.2 | async-start | bytes 25264128 | tf_op jit(solution)/shard_map/all_gather | solution.py:55
  12.9 43.3 %all-to-all-start = ((bf16[1,128,3,3072]{1,2,0,3:T(4,128)(2,1)}), bf16[1,128,3,3072]{1,2,0,3:T(4,128)(2,1)}, u32[]{:S(2)}, u32[]{:S(2)}) async-start(bf16[1,128,3,3072]{1,2,0,3:T(4,128)(2,1)} %copy.24), calls=%async_computation | async-start | bytes 6291456 | tf_op jit(solution)/shard_map/all_to_all | solution.py:40
  69.8 2.4 copy-start.2
  74.7 2.4 copy-start.2
  89.0 17.8 %all-to-all-start.1 = ((bf16[8,2,24576]{2,1,0:T(2,128)(2,1)}), bf16[8,2,24576]{2,1,0:T(2,128)(2,1)S(1)}, u32[]{:S(2)}, u32[]{:S(2)}) async-start(bf16[8,2,24576]{2,1,0:T(2,128)(2,1)} %reshape.13), calls=%async_computation.1 | async-start | bytes 1572864 | tf_op jit(solution)/shard_map/all_to_all | solution.py:46
  108.1 687.2 %copy-start.1 = (bf16[1,128,3072]{2,1,0:T(8,128)(2,1)S(1)}, bf16[1,128,3072]{2,1,0:T(8,128)(2,1)}, u32[]{:S(2)}) copy-start(bf16[1,128,3072]{2,1,0:T(8,128)(2,1)} %param.8) | copy-start | bytes 2359300
Sparse Core Ops, SparseCore 0:
  9.2 759.9 all-gather.2
where the time goes:
time: 828 us; the launch traced here: 812 us
  waiting for transfers between devices  711 us (86%)
  local copies, waits for them, and re-layouts  52.5 us (6%)
  matrix products  15.3 us (2%)
  between operations  14.1 us (2%)
  starting transfers between devices  10.5 us (1%)
    all_gather x1, waiting for transfers between devices, shards(): lax.all_gather(out_weight, ('tm', 'seq'), axis=0, tiled=True)  661 us
    all_to_all x1, waiting for transfers between devices, shards(): lax.all_to_all(projected, 'seq', split_axis=3, concat_axis=1, tiled=True)  38.1 us
    unnamed x10, local copies, waits for them, and re-layouts  34.2 us
  transfers between devices with their start and end apart: 3, of which 3 were waited for; matrix products, arithmetic and copies ran while one was open for 5% of the time, Pallas kernels for 0%

commit v1 on v0

v1 whole, which is shorter than its diff:
```python
import functools
import math

import jax
import jax.numpy as jnp
from jax import lax
from jax.experimental import pallas as pl
from jax.experimental.pallas import tpu as pltpu
from jax.sharding import PartitionSpec as P

MESH = pl.DeviceIdType.MESH
HD = 128
NH = 3
NS = 8
TOK = 128
QCOLS = 768
ROWS = 96
QBLK = 256
NCOL = 256


def coords():
    tm, s = lax.axis_index("tm"), lax.axis_index("seq")
    core = lax.rem(tm, 2)
    y = lax.rem(lax.div(tm, 2), 4)
    z = lax.div(tm, 8) * 2 + lax.rem(s, 2)
    return lax.div(s, 2), y, z, core


def device(x, y, z, core):
    return (lax.div(z, 2) * 8 + y * 2 + core, x * 2 + lax.rem(z, 2))


def kernel(
    proj, w_ref, out_ref,
    qkv, held, att, wpad, raw, wbuf, prod,
    first_send, first_recv, qkv_send, qkv_recv, z_send, z_recv, y_send, y_recv,
    relay_send, relay_recv, att_send, att_recv, pair_send, pair_recv, ret_send, ret_recv,
):
    x, y, z, core = coords()
    s = lax.axis_index("seq")
    zl = lax.rem(z, 2)
    zbase = z - zl
    twin = 1 - core
    xbit = lax.rem(x, 2)
    xother = x + 1 - 2 * xbit
    up = lax.rem(y + 1, 4)
    down = lax.rem(y + 3, 4)
    zup = lax.rem(z + 1, 8)
    zdown = lax.rem(z + 7, 8)

    def remote(src, dst, send, recv, target):
        return pltpu.make_async_remote_copy(
            src_ref=src, dst_ref=dst, send_sem=send, recv_sem=recv,
            device_id=target, device_id_type=MESH,
        )

    barrier = pltpu.get_barrier_semaphore()
    peers = []
    for c in (core, twin):
        for d in range(NS):
            if c is core and d == 0:
                continue
            other = lax.rem(s + d, NS)
            peers.append(device(lax.div(other, 2), y, zbase + lax.rem(other, 2), c))
    zouter = lax.rem(z + 7 + 2 * zl, 8)
    peers.append(device(x, y, zouter, core))
    peers.append(device(x, up, z, core))
    peers.append(device(x, down, z, core))
    for peer in peers:
        pl.semaphore_signal(barrier, inc=1, device_id=peer, device_id_type=MESH)

    wpad[...] = jnp.zeros_like(wpad)
    wpad[0:12, :] = w_ref[...]
    pl.semaphore_wait(barrier, len(peers))

    for k in range(NS):
        xt, ct = k // 2, k % 2
        quarter = (xt % 2) * 2 + ct
        src = wpad.at[:, pl.ds(quarter * QCOLS, QCOLS)]
        own = (x == xt) & (core == ct) & (zl == core)

        @pl.when(own)
        def _():
            pltpu.make_async_copy(src, raw.at[s], first_recv.at[s]).start()

        @pl.when(jnp.logical_not(own))
        def _():
            remote(
                src, raw.at[s], first_send.at[k], first_recv.at[s],
                device(jnp.int32(xt), y, zbase + core, jnp.int32(ct)),
            ).start()

    def qkv_copy(h, d):
        other = lax.rem(s + d, NS)
        col = pl.multiple_of((NS * h + other) * HD, HD)
        src = proj.at[:, :, pl.ds(col, HD)]
        dst = qkv.at[h, :, pl.ds(pl.multiple_of(s * TOK, TOK), TOK), :]
        if d == 0:
            return pltpu.make_async_copy(src, dst, qkv_recv.at[h])
        target = device(lax.div(other, 2), y, zbase + lax.rem(other, 2), core)
        return remote(src, dst, qkv_send.at[h * NS + d], qkv_recv.at[h], target)

    for h in range(NH):
        for d in range(NS):
            qkv_copy(h, d).start()

    for k in range(NS):
        pltpu.make_async_copy(raw.at[k], raw.at[k], first_recv.at[k]).wait()
    row = lax.broadcasted_iota(jnp.int32, (ROWS, 128), 0)
    col = lax.broadcasted_iota(jnp.int32, (ROWS, 128), 1)
    piece = lax.div(row, 12)
    pick = (col == piece * 16 + (row - piece * 12)).astype(jnp.float32).astype(jnp.bfloat16)
    tile = jnp.dot(
        pick, raw[...].reshape(128, QCOLS), preferred_element_type=jnp.float32
    ).astype(jnp.bfloat16)

    def tile_row(ty, tz):
        return pl.multiple_of((lax.div(tz, 2) * 8 + ty * 2 + lax.rem(tz, 2)) * ROWS, 32)

    wbuf[pl.ds(tile_row(y, z), ROWS), :] = tile

    order = [0, -1, 1, -2, 2, -3, 3, -4]

    def slot(ty, off, lo=0, n=ROWS):
        return wbuf.at[pl.ds(pl.multiple_of(tile_row(ty, lax.rem(z + off + 8, 8)) + lo, 16), n), :]

    def z_copy(off_at_sender):
        going_up, hops = off_at_sender
        off = -hops if going_up else hops
        ref = slot(y, off)
        k = hops if going_up else 4 + hops
        return remote(
            ref, ref, z_send.at[k], z_recv.at[k],
            device(x, y, zup if going_up else zdown, core),
        )

    def z_wait(going_up, hops):
        ref = slot(y, -(hops + 1) if going_up else hops + 1)
        k = hops if going_up else 4 + hops
        pltpu.make_async_copy(ref, ref, z_recv.at[k]).wait()

    def y_copy(i, going_up):
        ref = slot(y, order[i])
        k = 2 * i + (0 if going_up else 1)
        return remote(
            ref, ref, y_send.at[k], y_recv.at[k], device(x, up if going_up else down, z, core)
        )

    def relay_copy(i, going_up):
        ref = slot(down if going_up else up, order[i], 0 if going_up else 48, 48)
        k = 2 * i + (0 if going_up else 1)
        return remote(
            ref, ref, relay_send.at[k], relay_recv.at[k],
            device(x, up if going_up else down, z, core),
        )

    def share(i):
        y_copy(i, True).start()
        y_copy(i, False).start()

    def relay(i):
        for going_up in (True, False):
            ref = slot(down if going_up else up, order[i])
            pltpu.make_async_copy(ref, ref, y_recv.at[2 * i + (0 if going_up else 1)]).wait()
            relay_copy(i, going_up).start()

    def z_step(hops):
        z_wait(True, hops - 1)
        if hops < 4:
            z_copy((True, hops)).start()
        share(2 * hops - 1)
        if hops < 4:
            z_wait(False, hops - 1)
            if hops < 3:
                z_copy((False, hops)).start()
            share(2 * hops)

    z_copy((True, 0)).start()
    z_copy((False, 0)).start()
    share(0)

    def attend(h):
        ref = qkv.at[h]
        pltpu.make_async_copy(ref, ref, qkv_recv.at[h]).wait()
        factor = math.log2(math.e) / math.sqrt(HD)

        @pl.loop(0, NS * TOK // QBLK)
        def _(i):
            q = qkv[h, 0, pl.ds(pl.multiple_of(i * QBLK, QBLK), QBLK), :]
            scores = lax.dot_general(
                q, qkv[h, 1], (((1,), (1,)), ((), ())), preferred_element_type=jnp.float32
            ) * factor
            weights = jnp.exp2(scores - jnp.max(scores, axis=1, keepdims=True))
            totals = jnp.sum(weights, axis=1, keepdims=True)
            summed = jnp.dot(
                weights.astype(jnp.bfloat16), qkv[h, 2], preferred_element_type=jnp.float32
            )
            res = (summed / totals).astype(jnp.bfloat16).reshape(1, 1, 2, TOK, HD)
            held[pl.ds(h, 1), pl.ds(lax.div(i, 2), 1), pl.ds(lax.rem(i, 2), 1)] = res[None]

        for d in range(NS):
            att_copy(h, d).start()

    def att_copy(h, d):
        other = lax.rem(s + d, NS)
        src = held.at[h, lax.div(other, 4), :, lax.rem(other, 2)]
        dst = att.at[h, core, :, :, pl.ds(pl.multiple_of(s * HD, HD), HD)]
        if d == 0:
            return pltpu.make_async_copy(src, dst, att_recv.at[h])
        target = device(lax.div(other, 2), y, zbase + lax.rem(other, 2), core)
        return remote(src, dst, att_send.at[h * NS + d], att_recv.at[h], target)

    def pair_copy(h):
        ref = att.at[h, core]
        return remote(ref, ref, pair_send.at[h], pair_recv.at[h], device(x, y, z, twin))

    def pair(h):
        ref = att.at[h, core]
        pltpu.make_async_copy(ref, ref, att_recv.at[h]).wait()
        pair_copy(h).start()

    z_step(1)
    relay(0)
    attend(0)
    z_step(2)
    relay(1)
    relay(2)
    attend(1)
    pair(0)
    z_step(3)
    z_step(4)
    relay(3)
    relay(4)
    attend(2)
    pair(1)
    relay(5)
    relay(6)
    pair(2)
    relay(7)
    for i in range(8):
        for going_up in (True, False):
            ref = slot(lax.rem(y + 2, 4), order[i], 0 if going_up else 48, 48)
            pltpu.make_async_copy(ref, ref, relay_recv.at[2 * i + (0 if going_up else 1)]).wait()
    for h in range(NH):
        ref = att.at[h, twin]
        pltpu.make_async_copy(ref, ref, pair_recv.at[h]).wait()

    quarter = (xbit * 2 + core) * QCOLS

    def product(bit, n):
        total = None
        for h in range(NH):
            left = att[h, :, pl.ds(bit, 1)].reshape(2 * TOK, NS * HD)
            term = jnp.dot(
                left, wbuf[h * NS * HD:(h + 1) * NS * HD, n * NCOL:(n + 1) * NCOL],
                preferred_element_type=jnp.float32,
            )
            total = term if total is None else total + term
        return total.astype(jnp.bfloat16).reshape(2, 1, TOK, NCOL)

    def ret_copy(n, blk, far):
        cols = pl.ds(n * NCOL, NCOL)
        to = pl.ds(pl.multiple_of(quarter + n * NCOL, NCOL), NCOL)
        src = prod.at[blk, (1 - xbit) if far else xbit, :, cols]
        dst = out_ref.at[:, to]
        k = (0 if blk is core else 1) + (0 if far else 2)
        if not far and blk is core:
            return pltpu.make_async_copy(src, dst, ret_recv.at[k * 3 + n])
        return remote(
            src, dst, ret_send.at[k * 3 + n], ret_recv.at[k * 3 + n],
            device(xother if far else x, y, z, blk),
        )

    for far in (True, False):
        bit = 1 - xbit if far else xbit
        for n in range(QCOLS // NCOL):
            prod[:, pl.ds(bit, 1), :, n * NCOL:(n + 1) * NCOL] = product(bit, n)
            for blk in (core, twin):
                ret_copy(n, blk, far).start()

    for n in range(QCOLS // NCOL):
        for far in (True, False):
            for blk in (core, twin):
                c = ret_copy(n, blk, far)
                if far or blk is twin:
                    c.wait_send()
        for far in (True, False):
            for blk in (core, twin):
                k = (0 if blk is core else 1) + (0 if far else 2)
                fq = ((1 - xbit if far else xbit) * 2 + blk) * QCOLS + n * NCOL
                ref = out_ref.at[:, pl.ds(pl.multiple_of(fq, NCOL), NCOL)]
                pltpu.make_async_copy(ref, ref, ret_recv.at[k * 3 + n]).wait()
    for k in range(NS):
        own = (x == k // 2) & (core == k % 2) & (zl == core)

        @pl.when(jnp.logical_not(own))
        def _():
            remote(
                wpad.at[:, pl.ds(0, QCOLS)], raw.at[s], first_send.at[k], first_recv.at[s],
                device(jnp.int32(k // 2), y, zbase + core, jnp.int32(k % 2)),
            ).wait_send()

    for h in range(NH):
        for d in range(1, NS):
            qkv_copy(h, d).wait_send()
            att_copy(h, d).wait_send()
        pair_copy(h).wait_send()
    for hops in range(4):
        z_copy((True, hops)).wait_send()
        if hops < 3:
            z_copy((False, hops)).wait_send()
    for i in range(8):
        for going_up in (True, False):
            y_copy(i, going_up).wait_send()
            relay_copy(i, going_up).wait_send()


def project(proj, w):
    bf = jnp.bfloat16
    dma = pltpu.SemaphoreType.DMA
    return pl.pallas_call(
        kernel,
        out_shape=jax.ShapeDtypeStruct((TOK, 4 * QCOLS), bf),
        in_specs=[pl.BlockSpec(memory_space=pl.ANY), pl.BlockSpec(memory_space=pltpu.VMEM)],
        out_specs=pl.BlockSpec(memory_space=pltpu.VMEM),
        scratch_shapes=[
            pltpu.VMEM((NH, 3, NS * TOK, HD), bf),
            pltpu.VMEM((NH, 2, 2, 2, TOK, HD), bf),
            pltpu.VMEM((NH, 2, 2, TOK, NS * HD), bf),
            pltpu.VMEM((16, 4 * QCOLS), bf),
            pltpu.VMEM((NS, 16, QCOLS), bf),
            pltpu.VMEM((32 * ROWS, QCOLS), bf),
            pltpu.VMEM((2, 2, TOK, QCOLS), bf),
            dma((NS,)), dma((NS,)),
            dma((NH * NS,)), dma((NH,)),
            dma((7,)), dma((7,)),
            dma((16,)), dma((16,)),
            dma((16,)), dma((16,)),
            dma((NH * NS,)), dma((NH,)),
            dma((NH,)), dma((NH,)),
            dma((12,)), dma((12,)),
        ],
        compiler_params=pltpu.CompilerParams(
            collective_id=0, has_side_effects=True, vmem_limit_bytes=40 << 20
        ),
        name="attend_project",
    )(proj, w)


def shards(projected, residual, timesteps, gate_table, out_weight):
    product = project(projected[0].transpose(1, 0, 2), out_weight)
    gate = lax.dynamic_slice(gate_table, (timesteps[0], 0), (1, gate_table.shape[1]))
    result = residual[0].astype(jnp.float32) + gate * product.astype(jnp.float32)
    return result.astype(jnp.bfloat16)[None]


def solution(mesh):
    placed = (
        P("tm", "seq", None, None),
        P("tm", "seq", None),
        P("tm"),
        P(),
        P(("tm", "seq"), None),
    )
    return jax.shard_map(
        shards, mesh=mesh, in_specs=placed, out_specs=P("tm", "seq", None), check_vma=False
    )
```

time: 828 us -> 93.3 us (0.11); the launches traced: 812 us -> 93.1 us
  waiting for transfers between devices: 711 us -> 0 us
  Pallas kernels: 0 us -> 88.3 us
  local copies, waits for them, and re-layouts: 52.5 us -> 2.96 us
  matrix products: 15.3 us -> 0 us
  between operations: 14.1 us -> 0.75 us
  starting transfers between devices: 10.5 us -> 0 us
    all_gather x1 -> x0, waiting for transfers between devices: 661 us -> none  [shards(): lax.all_gather(out_weight, ('tm', 'seq'), axis=0, tiled=True)]
    pallas_call x0 -> x1, Pallas kernels: none -> 88.3 us  [project(): pl.pallas_call(kernel, out_shape=jax.ShapeDtypeStruct((TOK, 4 * QCOLS), b...]
    all_to_all x2 -> x0, waiting for transfers between devices: 49.6 us -> none  [the longest x1 38.1 us: shards(): lax.all_to_all(projected, 'seq', split_axis=3, concat_axis=1, tiled=True)]
    unnamed x10 -> x8, local copies, waits for them, and re-layouts: 34.2 us -> 2.95 us
    dot_general x6 -> x0, matrix products: 15.3 us -> none  [the longest x1 9.9 us: shards(): jnp.dot(back, lax.all_gather(out_weight, ('tm', 'seq'), axis=0, tiled=Tru...]
    all_to_all x2 -> x0, starting transfers between devices: 10.5 us -> none  [the longest x1 5.29 us: shards(): lax.all_to_all(attended.reshape(1, seq_len, attended.shape[1]), 'seq', sp...]
  transfers between devices with their start and end apart: 3 -> 0, of which waited for: 3 -> 0; matrix products, arithmetic and copies ran while one was open for 5% -> 0% of each run, Pallas kernels for 0% -> 0%
where the time goes in v1:
time: 93.3 us; the launch traced here: 93.1 us
  Pallas kernels  88.3 us (95%)
  local copies, waits for them, and re-layouts  2.96 us (3%)
  other arithmetic  1.12 us (1%)
    pallas_call x1, Pallas kernels, project(): pl.pallas_call(kernel, out_shape=jax.ShapeDtypeStruct((TOK, 4 * QCOLS), b...  88.3 us
    unnamed x8, local copies, waits for them, and re-layouts  2.95 us

profile of v1, /device:TPU:33, one launch (start us, length us, event | category | flops | bytes accessed | tf_op | source)
XLA Modules:
  0.0 93.1 jit_solution(17528201558425659140)
XLA Ops:
  0.0 0.0 copy-start
  0.7 0.4 copy-done
  1.1 0.0 copy-start.1
  1.1 1.7 %copy-done.1 = bf16[1,128,3,3072]{3,1,2,0:T(8,128)(2,1)S(1)} copy-done((bf16[1,128,3,3072]{3,1,2,0:T(8,128)(2,1)S(1)}, bf16[1,128,3,3072]{3,1,2,0:T(8,128)(2,1)}, u32[]{:S(2)}) %copy-start.1) | copy-done | bytes 2359320
  2.8 0.0 copy-start.2
  2.8 0.9 copy-done.2
  3.7 0.0 copy-start.3
  3.7 88.3 %attend_project.1 = bf16[128,3072]{1,0:T(8,128)(2,1)S(1)} custom-call(bf16[3,128,3072]{2,1,0:T(8,128)(2,1)S(1)} %bitcast.13, bf16[12,3072]{1,0:T(8,128)(2,1)S(1)} %copy-done.2), custom_call_target="tpu_custom_call" | custom-call | tf_op jit(solution)/shard_map/attend_project/pallas_call | solution.py:322
  92.0 0.0 copy-done.3
  92.0 1.1 %fusion.1 = bf16[1,128,3072]{2,1,0:T(8,128)(2,1)} fusion(bf16[128,3072]{1,0:T(8,128)(2,1)S(1)} %attend_project.1, bf16[1,128,3072]{2,1,0:T(8,128)(2,1)S(1)} %copy-done.3, f32[3072]{0:T(1024)S(1)} %bitcast.14), kind=kLoop, calls=%fused_computation.2 | loop fusion | flops 1966080 | bytes 2371584 | tf_op jit(solution)/shard_map/broadcast_in_dim | solution.py:355
  (1 shorter events, 0.0 us)
Async XLA Ops:
  0.0 1.1 %copy-start = (f32[50,3072]{1,0:T(8,128)S(1)}, f32[50,3072]{1,0:T(8,128)}, u32[]{:S(2)}) copy-start(f32[50,3072]{1,0:T(8,128)} %param.8) | copy-start | bytes 1843204
  1.1 1.7 %copy-start.1 = (bf16[1,128,3,3072]{3,1,2,0:T(8,128)(2,1)S(1)}, bf16[1,128,3,3072]{3,1,2,0:T(8,128)(2,1)}, u32[]{:S(2)}) copy-start(bf16[1,128,3,3072]{3,1,2,0:T(8,128)(2,1)} %param.5) | copy-start | bytes 7077892
  2.8 0.9 copy-start.2
  3.7 88.3 %copy-start.3 = (bf16[1,128,3072]{2,1,0:T(8,128)(2,1)S(1)}, bf16[1,128,3072]{2,1,0:T(8,128)(2,1)}, u32[]{:S(2)}) copy-start(bf16[1,128,3072]{2,1,0:T(8,128)(2,1)} %param.6) | copy-start | bytes 2359300

commit v2 on v1

--- a/solution.py
+++ b/solution.py
@@ -35,7 +35,9 @@
     proj, w_ref, out_ref,
     qkv, held, att, wpad, raw, wbuf, prod,
     first_send, first_recv, qkv_send, qkv_recv, z_send, z_recv, y_send, y_recv,
-    relay_send, relay_recv, att_send, att_recv, pair_send, pair_recv, ret_send, ret_recv,
+    relay_send, relay_recv, att_send, att_recv, cross_send, cross_recv, hand_send, hand_recv,
+    last_send, last_recv, last_pair_send, last_pair_recv, pair_send, pair_recv, ret_send, ret_recv,
+    wown, load_sem, acc,
 ):
     x, y, z, core = coords()
     s = lax.axis_index("seq")
@@ -70,8 +72,11 @@
     for peer in peers:
         pl.semaphore_signal(barrier, inc=1, device_id=peer, device_id_type=MESH)
 
+    load = pltpu.make_async_copy(w_ref, wown, load_sem)
+    load.start()
     wpad[...] = jnp.zeros_like(wpad)
-    wpad[0:12, :] = w_ref[...]
+    load.wait()
+    wpad[0:12, :] = wown[...]
     pl.semaphore_wait(barrier, len(peers))
 
     for k in range(NS):
@@ -101,10 +106,17 @@
         target = device(lax.div(other, 2), y, zbase + lax.rem(other, 2), core)
         return remote(src, dst, qkv_send.at[h * NS + d], qkv_recv.at[h], target)
 
-    for h in range(NH):
-        for d in range(NS):
+    def same(h):
+        for d in (2, 6, 4, 0):
             qkv_copy(h, d).start()
 
+    def other(h):
+        for d in (1, 7, 3, 5):
+            qkv_copy(h, d).start()
+
+    other(0)
+    same(0)
+    same(1)
     for k in range(NS):
         pltpu.make_async_copy(raw.at[k], raw.at[k], first_recv.at[k]).wait()
     row = lax.broadcasted_iota(jnp.int32, (ROWS, 128), 0)
@@ -123,13 +135,12 @@
     order = [0, -1, 1, -2, 2, -3, 3, -4]
 
     def slot(ty, off, lo=0, n=ROWS):
-        return wbuf.at[pl.ds(pl.multiple_of(tile_row(ty, lax.rem(z + off + 8, 8)) + lo, 16), n), :]
-
-    def z_copy(off_at_sender):
-        going_up, hops = off_at_sender
-        off = -hops if going_up else hops
-        ref = slot(y, off)
-        k = hops if going_up else 4 + hops
+        first = tile_row(ty, lax.rem(z + off + 8, 8)) + lo
+        return wbuf.at[pl.ds(pl.multiple_of(first, 16), n), :]
+
+    def z_copy(going_up, hops):
+        ref = slot(y, -hops if going_up else hops)
+        k = (hops if going_up else 4 + hops)
         return remote(
             ref, ref, z_send.at[k], z_recv.at[k],
             device(x, y, zup if going_up else zdown, core),
@@ -137,7 +148,7 @@
 
     def z_wait(going_up, hops):
         ref = slot(y, -(hops + 1) if going_up else hops + 1)
-        k = hops if going_up else 4 + hops
+        k = (hops if going_up else 4 + hops)
         pltpu.make_async_copy(ref, ref, z_recv.at[k]).wait()
 
     def y_copy(i, going_up):
@@ -159,26 +170,42 @@
         y_copy(i, True).start()
         y_copy(i, False).start()
 
-    def relay(i):
-        for going_up in (True, False):
-            ref = slot(down if going_up else up, order[i])
-            pltpu.make_async_copy(ref, ref, y_recv.at[2 * i + (0 if going_up else 1)]).wait()
-            relay_copy(i, going_up).start()
+    def relay(*which):
+        for i in which:
+            for going_up in (True, False):
+                ref = slot(down if going_up else up, order[i])
+                k = 2 * i + (0 if going_up else 1)
+                pltpu.make_async_copy(ref, ref, y_recv.at[k]).wait()
+                relay_copy(i, going_up).start()
+
+    def relayed():
+        for i in range(8):
+            for going_up in (True, False):
+                ref = slot(lax.rem(y + 2, 4), order[i], 0 if going_up else 48, 48)
+                k = 2 * i + (0 if going_up else 1)
+                pltpu.make_async_copy(ref, ref, relay_recv.at[k]).wait()
 
     def z_step(hops):
         z_wait(True, hops - 1)
         if hops < 4:
-            z_copy((True, hops)).start()
+            z_copy(True, hops).start()
         share(2 * hops - 1)
         if hops < 4:
             z_wait(False, hops - 1)
             if hops < 3:
-                z_copy((False, hops)).start()
+                z_copy(False, hops).start()
             share(2 * hops)
 
-    z_copy((True, 0)).start()
-    z_copy((False, 0)).start()
-    share(0)
+    def z_first():
+        z_copy(True, 0).start()
+        z_copy(False, 0).start()
+        share(0)
+
+    z_first()
+    other(1)
+    same(2)
+
+    last = NH - 1
 
     def attend(h):
         ref = qkv.at[h]
@@ -199,66 +226,134 @@
             res = (summed / totals).astype(jnp.bfloat16).reshape(1, 1, 2, TOK, HD)
             held[pl.ds(h, 1), pl.ds(lax.div(i, 2), 1), pl.ds(lax.rem(i, 2), 1)] = res[None]
 
-        for d in range(NS):
-            att_copy(h, d).start()
-
-    def att_copy(h, d):
-        other = lax.rem(s + d, NS)
-        src = held.at[h, lax.div(other, 4), :, lax.rem(other, 2)]
-        dst = att.at[h, core, :, :, pl.ds(pl.multiple_of(s * HD, HD), HD)]
-        if d == 0:
+        if h < last:
+            for k in (0, 1):
+                cross_copy(h, k).start()
+            for k in (1, 3, 2, 0):
+                own_copy(h, k).start()
+        else:
+            for far in (True, False):
+                for d in (1, 7, 3, 5, 2, 6, 4, 0):
+                    piece_copy(d, far).start()
+
+    mine = pl.ds(pl.multiple_of(s * HD, HD), HD)
+
+    def own_copy(h, k):
+        xt = lax.rem(x + k, 4)
+        src = held.at[h, lax.div(xt, 2), :, zl]
+        dst = att.at[h, core, :, :, mine]
+        if k == 0:
             return pltpu.make_async_copy(src, dst, att_recv.at[h])
-        target = device(lax.div(other, 2), y, zbase + lax.rem(other, 2), core)
-        return remote(src, dst, att_send.at[h * NS + d], att_recv.at[h], target)
+        return remote(src, dst, att_send.at[h * 4 + k], att_recv.at[h], device(xt, y, z, core))
+
+    def cross_copy(h, k):
+        xt = x if k == 0 else 3 - x
+        src = held.at[h, lax.div(xt, 2), :, 1 - zl]
+        dst = att.at[h, core, :, :, mine]
+        return remote(
+            src, dst, cross_send.at[h * 2 + k], cross_recv.at[h],
+            device(xt, y, zbase + 1 - zl, core),
+        )
+
+    def hand_copy(h, k):
+        xt = x if k == 0 else 3 - x
+        cols = pl.ds(pl.multiple_of((xt * 2 + 1 - zl) * HD, HD), HD)
+        ref = att.at[h, core, :, :, cols]
+        return remote(
+            ref, ref, hand_send.at[h * 2 + k], hand_recv.at[h], device(xother, y, z, core)
+        )
+
+    def hand(h):
+        ref = att.at[h, core, :, :, pl.ds(0, 2 * HD)]
+        pltpu.make_async_copy(ref, ref, cross_recv.at[h]).wait()
+        hand_copy(h, 0).start()
+        hand_copy(h, 1).start()
 
     def pair_copy(h):
         ref = att.at[h, core]
         return remote(ref, ref, pair_send.at[h], pair_recv.at[h], device(x, y, z, twin))
 
     def pair(h):
-        ref = att.at[h, core]
+        ref = att.at[h, core, :, :, pl.ds(0, 4 * HD)]
         pltpu.make_async_copy(ref, ref, att_recv.at[h]).wait()
+        ref = att.at[h, core, :, :, pl.ds(0, 2 * HD)]
+        pltpu.make_async_copy(ref, ref, hand_recv.at[h]).wait()
         pair_copy(h).start()
+
+    def piece_copy(d, far):
+        to = lax.rem(s + d, NS)
+        bit = lax.rem(lax.div(to, 2), 2)
+        bit = 1 - bit if far else bit
+        k = 0 if far else 1
+        src = held.at[last, lax.div(to, 4), bit, lax.rem(to, 2)]
+        dst = att.at[last, core, bit, :, mine]
+        if d == 0:
+            return pltpu.make_async_copy(src, dst, last_recv.at[k])
+        target = device(lax.div(to, 2), y, zbase + lax.rem(to, 2), core)
+        return remote(src, dst, last_send.at[k * NS + d], last_recv.at[k], target)
+
+    def last_pair_copy(far):
+        ref = att.at[last, core, 1 - xbit if far else xbit]
+        k = 0 if far else 1
+        return remote(
+            ref, ref, last_pair_send.at[k], last_pair_recv.at[k], device(x, y, z, twin)
+        )
+
+    def last_pair(far):
+        k = 0 if far else 1
+        ref = att.at[last, core, 1 - xbit if far else xbit]
+        pltpu.make_async_copy(ref, ref, last_recv.at[k]).wait()
+        last_pair_copy(far).start()
+
+    def last_paired(far):
+        k = 0 if far else 1
+        ref = att.at[last, twin, 1 - xbit if far else xbit]
+        pltpu.make_async_copy(ref, ref, last_pair_recv.at[k]).wait()
+
+    quarter = (xbit * 2 + core) * QCOLS
+
+    def term(h, bit, n):
+        left = att[h, :, pl.ds(bit, 1)].reshape(2 * TOK, NS * HD)
+        return jnp.dot(
+            left, wbuf[h * NS * HD:(h + 1) * NS * HD, n * NCOL:(n + 1) * NCOL],
+            preferred_element_type=jnp.float32,
+        )
+
+    def paired(h):
+        ref = att.at[h, twin]
+        pltpu.make_async_copy(ref, ref, pair_recv.at[h]).wait()
+
+    def gather(h):
+        paired(h)
+        for far in (True, False):
+            bit = 1 - xbit if far else xbit
+            for n in range(QCOLS // NCOL):
+                at = (0 if far else 1, slice(None), slice(n * NCOL, (n + 1) * NCOL))
+                acc[at] = term(h, bit, n) if h == 0 else acc[at] + term(h, bit, n)
 
     z_step(1)
     relay(0)
+    other(2)
+    relay(1)
+    z_step(2)
     attend(0)
-    z_step(2)
-    relay(1)
     relay(2)
     attend(1)
-    pair(0)
     z_step(3)
-    z_step(4)
+    hand(0)
     relay(3)
     relay(4)
     attend(2)
-    pair(1)
+    z_step(4)
     relay(5)
     relay(6)
-    pair(2)
+    pair(0)
+    hand(1)
     relay(7)
-    for i in range(8):
-        for going_up in (True, False):
-            ref = slot(lax.rem(y + 2, 4), order[i], 0 if going_up else 48, 48)
-            pltpu.make_async_copy(ref, ref, relay_recv.at[2 * i + (0 if going_up else 1)]).wait()
-    for h in range(NH):
-        ref = att.at[h, twin]
-        pltpu.make_async_copy(ref, ref, pair_recv.at[h]).wait()
-
-    quarter = (xbit * 2 + core) * QCOLS
-
-    def product(bit, n):
-        total = None
-        for h in range(NH):
-            left = att[h, :, pl.ds(bit, 1)].reshape(2 * TOK, NS * HD)
-            term = jnp.dot(
-                left, wbuf[h * NS * HD:(h + 1) * NS * HD, n * NCOL:(n + 1) * NCOL],
-                preferred_element_type=jnp.float32,
-            )
-            total = term if total is None else total + term
-        return total.astype(jnp.bfloat16).reshape(2, 1, TOK, NCOL)
-
+    pair(1)
+    relayed()
+    gather(0)
+    gather(1)
     def ret_copy(n, blk, far):
         cols = pl.ds(n * NCOL, NCOL)
         to = pl.ds(pl.multiple_of(quarter + n * NCOL, NCOL), NCOL)
@@ -274,17 +369,22 @@
 
     for far in (True, False):
         bit = 1 - xbit if far else xbit
+        last_pair(far)
+        last_paired(far)
         for n in range(QCOLS // NCOL):
-            prod[:, pl.ds(bit, 1), :, n * NCOL:(n + 1) * NCOL] = product(bit, n)
+            total = acc[0 if far else 1, :, n * NCOL:(n + 1) * NCOL] + term(last, bit, n)
+            prod[:, pl.ds(bit, 1), :, n * NCOL:(n + 1) * NCOL] = (
+                total.astype(jnp.bfloat16).reshape(2, 1, TOK, NCOL)
+            )
             for blk in (core, twin):
                 ret_copy(n, blk, far).start()
+
 
     for n in range(QCOLS // NCOL):
         for far in (True, False):
             for blk in (core, twin):
-                c = ret_copy(n, blk, far)
                 if far or blk is twin:
-                    c.wait_send()
+                    ret_copy(n, blk, far).wait_send()
         for far in (True, False):
             for blk in (core, twin):
                 k = (0 if blk is core else 1) + (0 if far else 2)
@@ -304,12 +404,21 @@
     for h in range(NH):
         for d in range(1, NS):
             qkv_copy(h, d).wait_send()
-            att_copy(h, d).wait_send()
+    for h in range(last):
+        for k in range(1, 4):
+            own_copy(h, k).wait_send()
+        for k in range(2):
+            cross_copy(h, k).wait_send()
+            hand_copy(h, k).wait_send()
         pair_copy(h).wait_send()
+    for far in (True, False):
+        for d in range(1, NS):
+            piece_copy(d, far).wait_send()
+        last_pair_copy(far).wait_send()
     for hops in range(4):
-        z_copy((True, hops)).wait_send()
+        z_copy(True, hops).wait_send()
         if hops < 3:
-            z_copy((False, hops)).wait_send()
+            z_copy(False, hops).wait_send()
     for i in range(8):
         for going_up in (True, False):
             y_copy(i, going_up).wait_send()
@@ -322,7 +431,7 @@
     return pl.pallas_call(
         kernel,
         out_shape=jax.ShapeDtypeStruct((TOK, 4 * QCOLS), bf),
-        in_specs=[pl.BlockSpec(memory_space=pl.ANY), pl.BlockSpec(memory_space=pltpu.VMEM)],
+        in_specs=[pl.BlockSpec(memory_space=pl.ANY), pl.BlockSpec(memory_space=pl.ANY)],
         out_specs=pl.BlockSpec(memory_space=pltpu.VMEM),
         scratch_shapes=[
             pltpu.VMEM((NH, 3, NS * TOK, HD), bf),
@@ -337,12 +446,18 @@
             dma((7,)), dma((7,)),
             dma((16,)), dma((16,)),
             dma((16,)), dma((16,)),
-            dma((NH * NS,)), dma((NH,)),
+            dma((NH * 4,)), dma((NH,)),
+            dma((NH * 2,)), dma((NH,)),
+            dma((NH * 2,)), dma((NH,)),
+            dma((2 * NS,)), dma((2,)),
+            dma((2,)), dma((2,)),
             dma((NH,)), dma((NH,)),
             dma((12,)), dma((12,)),
+            pltpu.VMEM((12, 4 * QCOLS), bf), dma,
+            pltpu.VMEM((2, 2 * TOK, QCOLS), jnp.float32),
         ],
         compiler_params=pltpu.CompilerParams(
-            collective_id=0, has_side_effects=True, vmem_limit_bytes=40 << 20
+            collective_id=0, has_side_effects=True, vmem_limit_bytes=62 << 20
         ),
         name="attend_project",
     )(proj, w)

time: 93.3 us -> 85.1 us (0.912)
  Pallas kernels: 88.3 us -> 81.5 us
  local copies, waits for them, and re-layouts: 2.96 us -> 0.41 us
  other arithmetic: 1.12 us -> 2.25 us
    pallas_call x1, Pallas kernels: 88.3 us -> 81.5 us  [project(): pl.pallas_call(kernel, out_shape=jax.ShapeDtypeStruct((TOK, 4 * QCOLS), b...]
    unnamed x8 -> x4, local copies, waits for them, and re-layouts: 2.95 us -> 0.4 us
    broadcast_in_dim x1, other arithmetic: 1.12 us -> 2.25 us  [shards(): return result.astype(jnp.bfloat16)[None]]
where the time goes in v2:
time: 85.1 us; the launch traced here: 85 us
  Pallas kernels  81.5 us (96%)
  other arithmetic  2.25 us (3%)
    pallas_call x1, Pallas kernels, project(): pl.pallas_call(kernel, out_shape=jax.ShapeDtypeStruct((TOK, 4 * QCOLS), b...  81.5 us
    broadcast_in_dim x1, other arithmetic, shards(): return result.astype(jnp.bfloat16)[None]  2.25 us

profile of v2, /device:TPU:33, one launch (start us, length us, event | category | flops | bytes accessed | tf_op | source)
XLA Modules:
  0.0 85.0 jit_solution(14640275659528755690)
XLA Ops:
  0.0 0.0 copy-start
  0.7 0.4 copy-done
  1.1 0.0 copy-start.1
  1.1 81.5 %attend_project.1 = bf16[128,3072]{1,0:T(8,128)(2,1)} custom-call(bf16[3,128,3072]{2,1,0:T(8,128)(2,1)} %bitcast.13, bf16[12,3072]{1,0:T(8,128)(2,1)} %w_ref.1), custom_call_target="tpu_custom_call" | custom-call | tf_op jit(solution)/shard_map/attend_project/pallas_call | solution.py:431
  82.7 0.0 copy-done.1
  82.7 2.3 %fusion.1 = bf16[1,128,3072]{2,1,0:T(8,128)(2,1)} fusion(bf16[128,3072]{1,0:T(8,128)(2,1)} %attend_project.1, bf16[1,128,3072]{2,1,0:T(8,128)(2,1)S(1)} %copy-done.1, f32[3072]{0:T(1024)S(1)} %bitcast.14), kind=kLoop, calls=%fused_computation.2 | loop fusion | flops 1966080 | bytes 2371584 | tf_op jit(solution)/shard_map/broadcast_in_dim | solution.py:470
  (1 shorter events, 0.0 us)
Async XLA Ops:
  0.0 1.1 %copy-start = (f32[50,3072]{1,0:T(8,128)S(1)}, f32[50,3072]{1,0:T(8,128)}, u32[]{:S(2)}) copy-start(f32[50,3072]{1,0:T(8,128)} %param.8) | copy-start | bytes 1843204
  1.1 81.6 %copy-start.1 = (bf16[1,128,3072]{2,1,0:T(8,128)(2,1)S(1)}, bf16[1,128,3072]{2,1,0:T(8,128)(2,1)}, u32[]{:S(2)}) copy-start(bf16[1,128,3072]{2,1,0:T(8,128)(2,1)} %param.6) | copy-start | bytes 2359300

commit v3 on v2

--- a/solution.py
+++ b/solution.py
@@ -110,8 +110,8 @@
         for d in (2, 6, 4, 0):
             qkv_copy(h, d).start()
 
-    def other(h):
-        for d in (1, 7, 3, 5):
+    def other(h, some=(1, 7, 3, 5)):
+        for d in some:
             qkv_copy(h, d).start()
 
     other(0)
@@ -339,16 +339,16 @@
     attend(0)
     relay(2)
     attend(1)
-    z_step(3)
-    hand(0)
     relay(3)
     relay(4)
+    z_step(3)
     attend(2)
+    hand(0)
     z_step(4)
     relay(5)
+    hand(1)
     relay(6)
     pair(0)
-    hand(1)
     relay(7)
     pair(1)
     relayed()
@@ -457,7 +457,7 @@
             pltpu.VMEM((2, 2 * TOK, QCOLS), jnp.float32),
         ],
         compiler_params=pltpu.CompilerParams(
-            collective_id=0, has_side_effects=True, vmem_limit_bytes=62 << 20
+            collective_id=0, has_side_effects=True, vmem_limit_bytes=53 << 20
         ),
         name="attend_project",
     )(proj, w)

time: 85.1 us -> 82.7 us (0.972)
  Pallas kernels: 81.5 us -> 79.4 us
  other arithmetic: 2.25 us -> 1.12 us
  local copies, waits for them, and re-layouts: 0.41 us -> 1.3 us
    pallas_call x1, Pallas kernels: 81.5 us -> 79.4 us  [project(): pl.pallas_call(kernel, out_shape=jax.ShapeDtypeStruct((TOK, 4 * QCOLS), b...]
    broadcast_in_dim x1, other arithmetic: 2.25 us -> 1.12 us  [shards(): return result.astype(jnp.bfloat16)[None]]
    unnamed x4 -> x6, local copies, waits for them, and re-layouts: 0.4 us -> 1.28 us
where the time goes in v3:
time: 82.7 us; the launch traced here: 82.6 us
  Pallas kernels  79.4 us (96%)
  local copies, waits for them, and re-layouts  1.3 us (2%)
  other arithmetic  1.12 us (1%)
    pallas_call x1, Pallas kernels, project(): pl.pallas_call(kernel, out_shape=jax.ShapeDtypeStruct((TOK, 4 * QCOLS), b...  79.4 us

profile of v3, /device:TPU:33, one launch (start us, length us, event | category | flops | bytes accessed | tf_op | source)
XLA Modules:
  0.0 82.6 jit_solution(5448346935483412944)
XLA Ops:
  0.0 0.0 copy-start
  0.7 0.4 copy-done
  1.1 0.0 copy-start.1
  1.1 0.9 %copy-done.1 = bf16[12,3072]{1,0:T(8,128)(2,1)S(1)} copy-done((bf16[12,3072]{1,0:T(8,128)(2,1)S(1)}, bf16[12,3072]{1,0:T(8,128)(2,1)}, u32[]{:S(2)}) %copy-start.1) | copy-done | bytes 73752
  2.0 0.0 copy-start.2
  2.0 79.4 %attend_project.1 = bf16[128,3072]{1,0:T(8,128)(2,1)S(1)} custom-call(bf16[3,128,3072]{2,1,0:T(8,128)(2,1)} %bitcast.13, bf16[12,3072]{1,0:T(8,128)(2,1)S(1)} %copy-done.1), custom_call_target="tpu_custom_call" | custom-call | tf_op jit(solution)/shard_map/attend_project/pallas_call | solution.py:431
  81.5 0.0 copy-done.2
  81.5 1.1 %fusion.1 = bf16[1,128,3072]{2,1,0:T(8,128)(2,1)} fusion(bf16[128,3072]{1,0:T(8,128)(2,1)S(1)} %attend_project.1, bf16[1,128,3072]{2,1,0:T(8,128)(2,1)S(1)} %copy-done.2, f32[3072]{0:T(1024)S(1)} %bitcast.14), kind=kLoop, calls=%fused_computation.2 | loop fusion | flops 1966080 | bytes 2371584 | tf_op jit(solution)/shard_map/broadcast_in_dim | solution.py:470
  (1 shorter events, 0.0 us)
Async XLA Ops:
  0.0 1.1 %copy-start = (f32[50,3072]{1,0:T(8,128)S(1)}, f32[50,3072]{1,0:T(8,128)}, u32[]{:S(2)}) copy-start(f32[50,3072]{1,0:T(8,128)} %param.8) | copy-start | bytes 1843204
  1.1 0.9 %copy-start.1 = (bf16[12,3072]{1,0:T(8,128)(2,1)S(1)}, bf16[12,3072]{1,0:T(8,128)(2,1)}, u32[]{:S(2)}) copy-start(bf16[12,3072]{1,0:T(8,128)(2,1)} %w_ref.1) | copy-start | bytes 221188
  2.0 79.4 %copy-start.2 = (bf16[1,128,3072]{2,1,0:T(8,128)(2,1)S(1)}, bf16[1,128,3072]{2,1,0:T(8,128)(2,1)}, u32[]{:S(2)}) copy-start(bf16[1,128,3072]{2,1,0:T(8,128)(2,1)} %param.6) | copy-start | bytes 2359300

commit v4 on v3

--- a/solution.py
+++ b/solution.py
@@ -325,11 +325,9 @@
 
     def gather(h):
         paired(h)
-        for far in (True, False):
-            bit = 1 - xbit if far else xbit
-            for n in range(QCOLS // NCOL):
-                at = (0 if far else 1, slice(None), slice(n * NCOL, (n + 1) * NCOL))
-                acc[at] = term(h, bit, n) if h == 0 else acc[at] + term(h, bit, n)
+        for n in range(QCOLS // NCOL):
+            at = (slice(None), slice(n * NCOL, (n + 1) * NCOL))
+            acc[at] = term(h, 1 - xbit, n) if h == 0 else acc[at] + term(h, 1 - xbit, n)
 
     z_step(1)
     relay(0)
@@ -372,7 +370,11 @@
         last_pair(far)
         last_paired(far)
         for n in range(QCOLS // NCOL):
-            total = acc[0 if far else 1, :, n * NCOL:(n + 1) * NCOL] + term(last, bit, n)
+            if far:
+                total = acc[:, n * NCOL:(n + 1) * NCOL]
+            else:
+                total = term(0, bit, n) + term(1, bit, n)
+            total = total + term(last, bit, n)
             prod[:, pl.ds(bit, 1), :, n * NCOL:(n + 1) * NCOL] = (
                 total.astype(jnp.bfloat16).reshape(2, 1, TOK, NCOL)
             )
@@ -454,7 +456,7 @@
             dma((NH,)), dma((NH,)),
             dma((12,)), dma((12,)),
             pltpu.VMEM((12, 4 * QCOLS), bf), dma,
-            pltpu.VMEM((2, 2 * TOK, QCOLS), jnp.float32),
+            pltpu.VMEM((2 * TOK, QCOLS), jnp.float32),
         ],
         compiler_params=pltpu.CompilerParams(
             collective_id=0, has_side_effects=True, vmem_limit_bytes=53 << 20

time: 82.7 us -> 82.1 us (level)
  no operation moved by 1% of the time
where the time goes in v4:
time: 82.1 us; the launch traced here: 82 us
  Pallas kernels  78.9 us (96%)
  local copies, waits for them, and re-layouts  1.3 us (2%)
  other arithmetic  1.12 us (1%)
    pallas_call x1, Pallas kernels, project(): pl.pallas_call(kernel, out_shape=jax.ShapeDtypeStruct((TOK, 4 * QCOLS), b...  78.9 us

profile of v4, /device:TPU:33, one launch (start us, length us, event | category | flops | bytes accessed | tf_op | source)
XLA Modules:
  0.0 82.0 jit_solution(14178452555565689706)
XLA Ops:
  0.0 0.0 copy-start
  0.7 0.4 copy-done
  1.1 0.0 copy-start.1
  1.1 0.9 %copy-done.1 = bf16[12,3072]{1,0:T(8,128)(2,1)S(1)} copy-done((bf16[12,3072]{1,0:T(8,128)(2,1)S(1)}, bf16[12,3072]{1,0:T(8,128)(2,1)}, u32[]{:S(2)}) %copy-start.1) | copy-done | bytes 73752
  2.0 0.0 copy-start.2
  2.0 78.9 %attend_project.1 = bf16[128,3072]{1,0:T(8,128)(2,1)S(1)} custom-call(bf16[3,128,3072]{2,1,0:T(8,128)(2,1)} %bitcast.13, bf16[12,3072]{1,0:T(8,128)(2,1)S(1)} %copy-done.1), custom_call_target="tpu_custom_call" | custom-call | tf_op jit(solution)/shard_map/attend_project/pallas_call | solution.py:433
  80.9 0.0 copy-done.2
  80.9 1.1 %fusion.1 = bf16[1,128,3072]{2,1,0:T(8,128)(2,1)} fusion(bf16[128,3072]{1,0:T(8,128)(2,1)S(1)} %attend_project.1, bf16[1,128,3072]{2,1,0:T(8,128)(2,1)S(1)} %copy-done.2, f32[3072]{0:T(1024)S(1)} %bitcast.14), kind=kLoop, calls=%fused_computation.2 | loop fusion | flops 1966080 | bytes 2371584 | tf_op jit(solution)/shard_map/broadcast_in_dim | solution.py:472
  (1 shorter events, 0.0 us)
Async XLA Ops:
  0.0 1.1 %copy-start = (f32[50,3072]{1,0:T(8,128)S(1)}, f32[50,3072]{1,0:T(8,128)}, u32[]{:S(2)}) copy-start(f32[50,3072]{1,0:T(8,128)} %param.8) | copy-start | bytes 1843204
  1.1 0.9 %copy-start.1 = (bf16[12,3072]{1,0:T(8,128)(2,1)S(1)}, bf16[12,3072]{1,0:T(8,128)(2,1)}, u32[]{:S(2)}) copy-start(bf16[12,3072]{1,0:T(8,128)(2,1)} %w_ref.1) | copy-start | bytes 221188
  2.0 78.9 %copy-start.2 = (bf16[1,128,3072]{2,1,0:T(8,128)(2,1)S(1)}, bf16[1,128,3072]{2,1,0:T(8,128)(2,1)}, u32[]{:S(2)}) copy-start(bf16[1,128,3072]{2,1,0:T(8,128)(2,1)} %param.6) | copy-start | bytes 2359300
